TPU v7x, 32 devices: a whole 2x2x4 slice. The times are simulated.
32 devices in a mesh: groups: 1, ctx: 32 (over z, y, x, core).
Axes of the slice: x: 2, y: 2, z: 4, core: 2. Of those that a mesh axis runs over, the one named last changes fastest.
Arguments:
- queries: bfloat16 [4096, 2048], P(('groups', 'ctx')), may hold values from -120 to 120
- self_keys: bfloat16 [4096, 2048], P(('groups', 'ctx')), may hold values from -6 to 6
- self_values: bfloat16 [4096, 2048], P(('groups', 'ctx')), may hold values from -6 to 6
- cross_queries: bfloat16 [4096, 2048], P(('groups', 'ctx')), may hold values from -6 to 6
- encoded: bfloat16 [4096, 896], P(('groups', 'ctx')), may hold values from -6 to 6
- neighbour_weight: bfloat16 [896, 4096], replicated, may hold values from -1 to 1
- counts: int32 [64], P(('groups', 'ctx')), may hold values from 0 to 2
- sources: int32 [64, 2], P(('groups', 'ctx')), may hold values from 0 to 61, as said below
Outputs:
- attended: bfloat16 [4096, 2048], P(('groups', 'ctx'))
Inputs may be any that keep to these rules, and one draw needn't show every extreme that they name: sources[c, j] equals max(c - 1 - r, 0) for some r with 1 <= r <= 29.
All inputs are finite; a program needn't handle non-finite values.
Results may differ from a plain program's by a relative error of at most 0.0061.
Values may be sent and summed in bfloat16 or wider, within the bound.
A program may use at most 128 MiB of HBM per device.

v0:
```python
import jax
import jax.numpy as jnp
from jax import lax
from jax.sharding import PartitionSpec as P

HEADS = 16
HEAD_DIM = 128
SPAN = 64
REACH = 16


MASKED_SCORE = -1e30


def shifted(value, axis, steps):
    count = lax.axis_size(axis)
    first, last = (max(0, -steps), min(count, count - steps))
    return lax.ppermute(value, axis, [(source, source + steps) for source in range(first, last)])


def masked_weights(scores, valid_mask, extra_total):
    masked = jnp.where(valid_mask, scores, MASKED_SCORE)
    largest = jnp.max(masked, axis=-1, keepdims=True)
    exponent = jnp.where(valid_mask, jnp.exp(masked - largest), 0.0)
    totals = jnp.sum(exponent, axis=-1, keepdims=True)
    return (exponent / (totals + extra_total)).astype(jnp.bfloat16)


def window_attention(window_rows, queries, position, head_count, head_size):
    token_count, model_width = queries.shape
    window_length = window_rows.shape[0]
    reach_blocks = window_length // token_count - 1
    scale_factor = head_size ** (-0.5)
    query_index = jnp.arange(token_count, dtype=jnp.int32)[:, None]
    key_index = jnp.arange(window_length, dtype=jnp.int32)[None, :]
    valid_mask = (
        (key_index > query_index)
        & (key_index <= query_index + reach_blocks * token_count)
        & (key_index >= (reach_blocks - position) * token_count)
    )
    group_size = 4
    group_width = group_size * head_size

    def one_group(group_index):
        column_start = group_index * group_width
        query_group = lax.dynamic_slice_in_dim(queries, column_start, group_width, 1).reshape(
            token_count, group_size, head_size
        )
        key_group = lax.dynamic_slice_in_dim(window_rows, column_start, group_width, 1).reshape(
            window_length, group_size, head_size
        )
        value_group = lax.dynamic_slice_in_dim(
            window_rows, model_width + column_start, group_width, 1
        ).reshape(window_length, group_size, head_size)
        scores = (
            jnp.einsum("rhd,ihd->hri", query_group, key_group, preferred_element_type=jnp.float32)
            * scale_factor
        )
        weights = masked_weights(scores, valid_mask[None], 0.0)
        result = jnp.einsum(
            "hri,ihd->rhd", weights, value_group, preferred_element_type=jnp.float32
        )
        return result.reshape(token_count, group_width)

    grouped = lax.map(one_group, jnp.arange(head_count // group_size, dtype=jnp.int32))
    return jnp.moveaxis(grouped, 0, 1).reshape(token_count, model_width)


def neighbour_attention(
    query_rows,
    count_rows,
    source_rows,
    window_rows,
    neighbour_weight,
    position,
    head_count,
    head_size,
    span_size,
):
    token_count, model_width = query_rows.shape
    span_count = count_rows.shape[0]
    window_length = window_rows.shape[0]
    reach_blocks = window_length // token_count - 1
    scale_factor = head_size ** (-0.5)
    first_span = (position - reach_blocks) * span_count
    encoder_rows = window_rows[:, 2 * model_width :]
    row_starts = ((source_rows - first_span) * span_size).reshape(-1)

    def take_rows(row_start):
        return lax.dynamic_slice_in_dim(encoder_rows, row_start, 2 * span_size, 0)

    picked = jax.vmap(take_rows)(row_starts)
    projected = jnp.dot(
        picked.reshape(-1, picked.shape[-1]), neighbour_weight, preferred_element_type=jnp.float32
    ).astype(jnp.bfloat16)
    projected = projected.reshape(span_count, 4 * span_size, 2 * model_width)
    neighbour_keys = projected[:, :, :model_width].reshape(
        span_count, 4 * span_size, head_count, head_size
    )
    neighbour_values = projected[:, :, model_width:].reshape(
        span_count, 4 * span_size, head_count, head_size
    )
    query_blocks = query_rows.reshape(span_count, span_size, head_count, head_size)
    scores = (
        jnp.einsum(
            "cqhd,ckhd->chqk", query_blocks, neighbour_keys, preferred_element_type=jnp.float32
        )
        * scale_factor
    )
    slot_index = jnp.arange(4 * span_size, dtype=jnp.int32) // (2 * span_size)
    valid_mask = (slot_index[None, :] < count_rows[:, None])[:, None, None, :]
    extra_total = jnp.where(count_rows > 0, 0.0, 1.0)[:, None, None, None]
    weights = masked_weights(scores, valid_mask, extra_total)
    result = jnp.einsum(
        "chqk,ckhd->cqhd", weights, neighbour_values, preferred_element_type=jnp.float32
    )
    return result.reshape(token_count, model_width)


def per_device(
    queries, self_keys, self_values, cross_queries, encoded, neighbour_weight, counts, sources
):
    span_size = SPAN
    position = lax.axis_index("ctx")
    own_rows = jnp.concatenate([self_keys, self_values, encoded], axis=1)
    collected = [own_rows]
    moving = own_rows
    for turn_index in range(REACH):
        moving = shifted(moving, "ctx", 1)
        collected.insert(0, moving)
    window_rows = jnp.concatenate(collected, axis=0)
    self_part = window_attention(window_rows, queries, position, HEADS, HEAD_DIM)
    incoming = shifted(cross_queries[:span_size], "ctx", -1)
    later_rows = jnp.concatenate([cross_queries[span_size:], incoming], axis=0)
    partial_rows = neighbour_attention(
        later_rows,
        counts,
        sources,
        window_rows,
        neighbour_weight,
        position,
        HEADS,
        HEAD_DIM,
        span_size,
    )
    arriving = shifted(partial_rows[-span_size:], "ctx", 1)
    cross_part = jnp.concatenate([arriving, partial_rows[:-span_size]], axis=0)
    return (self_part + cross_part).astype(jnp.bfloat16)


def solution(mesh):
    return jax.shard_map(
        per_device,
        mesh=mesh,
        in_specs=(
            P(("groups", "ctx"), None),
            P(("groups", "ctx"), None),
            P(("groups", "ctx"), None),
            P(("groups", "ctx"), None),
            P(("groups", "ctx"), None),
            P(),
            P(("groups", "ctx")),
            P(("groups", "ctx"), None),
        ),
        out_specs=P(("groups", "ctx"), None),
        check_vma=False,
    )
```

profile of v0, /device:TPU:7, one launch (start us, length us, event | category | flops | bytes accessed | tf_op | source)
XLA Modules:
  0.0 472.9 jit_solution(5283761414181430499)
XLA Ops:
  6.7 14.2 %collective-permute-done = bf16[128,4992]{0,1:T(8,128)(2,1)S(1)} collective-permute-done((bf16[128,4992]{0,1:T(8,128)(2,1)S(1)}, bf16[128,4992]{0,1:T(8,128)(2,1)S(1)}, u32[]{:S(2)}, u32[]{:S(2)}) %collective-permute-start) | collective-permute-done | bytes 1277984 | tf_op jit(solution)/shard_map/ppermute | solution.py:18
  27.1 14.2 %collective-permute-done.1 = bf16[128,4992]{0,1:T(8,128)(2,1)S(1)} collective-permute-done((bf16[128,4992]{0,1:T(8,128)(2,1)S(1)}, bf16[128,4992]{0,1:T(8,128)(2,1)S(1)}, u32[]{:S(2)}, u32[]{:S(2)}) %collective-permute-start.1) | collective-permute-done | bytes 1277984 | tf_op jit(solution)/shard_map/ppermute | solution.py:18
  48.6 14.2 %collective-permute-done.2 = bf16[128,4992]{0,1:T(8,128)(2,1)S(1)} collective-permute-done((bf16[128,4992]{0,1:T(8,128)(2,1)S(1)}, bf16[128,4992]{0,1:T(8,128)(2,1)S(1)}, u32[]{:S(2)}, u32[]{:S(2)}) %collective-permute-start.2) | collective-permute-done | bytes 1277984 | tf_op jit(solution)/shard_map/ppermute | solution.py:18
  70.0 14.2 %collective-permute-done.3 = bf16[128,4992]{0,1:T(8,128)(2,1)S(1)} collective-permute-done((bf16[128,4992]{0,1:T(8,128)(2,1)S(1)}, bf16[128,4992]{0,1:T(8,128)(2,1)S(1)}, u32[]{:S(2)}, u32[]{:S(2)}) %collective-permute-start.3) | collective-permute-done | bytes 1277984 | tf_op jit(solution)/shard_map/ppermute | solution.py:18
  91.4 14.2 %collective-permute-done.4 = bf16[128,4992]{0,1:T(8,128)(2,1)S(1)} collective-permute-done((bf16[128,4992]{0,1:T(8,128)(2,1)S(1)}, bf16[128,4992]{0,1:T(8,128)(2,1)S(1)}, u32[]{:S(2)}, u32[]{:S(2)}) %collective-permute-start.4) | collective-permute-done | bytes 1277984 | tf_op jit(solution)/shard_map/ppermute | solution.py:18
  112.8 14.2 %collective-permute-done.5 = bf16[128,4992]{0,1:T(8,128)(2,1)S(1)} collective-permute-done((bf16[128,4992]{0,1:T(8,128)(2,1)S(1)}, bf16[128,4992]{0,1:T(8,128)(2,1)S(1)}, u32[]{:S(2)}, u32[]{:S(2)}) %collective-permute-start.5) | collective-permute-done | bytes 1277984 | tf_op jit(solution)/shard_map/ppermute | solution.py:18
  134.3 14.2 %collective-permute-done.6 = bf16[128,4992]{0,1:T(8,128)(2,1)S(1)} collective-permute-done((bf16[128,4992]{0,1:T(8,128)(2,1)S(1)}, bf16[128,4992]{0,1:T(8,128)(2,1)S(1)}, u32[]{:S(2)}, u32[]{:S(2)}) %collective-permute-start.6) | collective-permute-done | bytes 1277984 | tf_op jit(solution)/shard_map/ppermute | solution.py:18
  155.7 14.2 %collective-permute-done.7 = bf16[128,4992]{0,1:T(8,128)(2,1)S(1)} collective-permute-done((bf16[128,4992]{0,1:T(8,128)(2,1)S(1)}, bf16[128,4992]{0,1:T(8,128)(2,1)S(1)}, u32[]{:S(2)}, u32[]{:S(2)}) %collective-permute-start.7) | collective-permute-done | bytes 1277984 | tf_op jit(solution)/shard_map/ppermute | solution.py:18
  177.2 14.2 %collective-permute-done.8 = bf16[128,4992]{0,1:T(8,128)(2,1)S(1)} collective-permute-done((bf16[128,4992]{0,1:T(8,128)(2,1)S(1)}, bf16[128,4992]{0,1:T(8,128)(2,1)S(1)}, u32[]{:S(2)}, u32[]{:S(2)}) %collective-permute-start.8) | collective-permute-done | bytes 1277984 | tf_op jit(solution)/shard_map/ppermute | solution.py:18
  198.6 14.2 %collective-permute-done.9 = bf16[128,4992]{0,1:T(8,128)(2,1)S(1)} collective-permute-done((bf16[128,4992]{0,1:T(8,128)(2,1)S(1)}, bf16[128,4992]{0,1:T(8,128)(2,1)S(1)}, u32[]{:S(2)}, u32[]{:S(2)}) %collective-permute-start.9) | collective-permute-done | bytes 1277984 | tf_op jit(solution)/shard_map/ppermute | solution.py:18
  220.0 14.2 %collective-permute-done.10 = bf16[128,4992]{0,1:T(8,128)(2,1)S(1)} collective-permute-done((bf16[128,4992]{0,1:T(8,128)(2,1)S(1)}, bf16[128,4992]{0,1:T(8,128)(2,1)S(1)}, u32[]{:S(2)}, u32[]{:S(2)}) %collective-permute-start.10) | collective-permute-done | bytes 1277984 | tf_op jit(solution)/shard_map/ppermute | solution.py:18
  241.5 14.2 %collective-permute-done.11 = bf16[128,4992]{0,1:T(8,128)(2,1)S(1)} collective-permute-done((bf16[128,4992]{0,1:T(8,128)(2,1)S(1)}, bf16[128,4992]{0,1:T(8,128)(2,1)S(1)}, u32[]{:S(2)}, u32[]{:S(2)}) %collective-permute-start.11) | collective-permute-done | bytes 1277984 | tf_op jit(solution)/shard_map/ppermute | solution.py:18
  262.9 14.2 %collective-permute-done.12 = bf16[128,4992]{0,1:T(8,128)(2,1)S(1)} collective-permute-done((bf16[128,4992]{0,1:T(8,128)(2,1)S(1)}, bf16[128,4992]{0,1:T(8,128)(2,1)S(1)}, u32[]{:S(2)}, u32[]{:S(2)}) %collective-permute-start.12) | collective-permute-done | bytes 1277984 | tf_op jit(solution)/shard_map/ppermute | solution.py:18
  278.2 6.2 %collective-permute-start.13 = (bf16[128,4992]{0,1:T(8,128)(2,1)S(1)}, bf16[128,4992]{0,1:T(8,128)(2,1)}, u32[]{:S(2)}, u32[]{:S(2)}) collective-permute-start(bf16[128,4992]{0,1:T(8,128)(2,1)S(1)} %collective-permute-done.12), channel_id=1, source_target_pairs={{0,1},{1,2},{2,3},{3,4},{4,5},{5,6},{6,7},{7,8},{8,9},{9,10},{10,1... | collective-permute-start | bytes 3833864 | tf_op jit(solution)/shard_map/ppermute | solution.py:18
  284.4 14.2 %collective-permute-done.13 = bf16[128,4992]{0,1:T(8,128)(2,1)} collective-permute-done((bf16[128,4992]{0,1:T(8,128)(2,1)S(1)}, bf16[128,4992]{0,1:T(8,128)(2,1)}, u32[]{:S(2)}, u32[]{:S(2)}) %collective-permute-start.13) | collective-permute-done | bytes 1277984 | tf_op jit(solution)/shard_map/ppermute | solution.py:18
  298.5 6.3 %collective-permute-start.14 = (bf16[128,4992]{0,1:T(8,128)(2,1)}, bf16[128,4992]{0,1:T(8,128)(2,1)}, u32[]{:S(2)}, u32[]{:S(2)}) collective-permute-start(bf16[128,4992]{0,1:T(8,128)(2,1)} %collective-permute-done.13), channel_id=1, source_target_pairs={{0,1},{1,2},{2,3},{3,4},{4,5},{5,6},{6,7},{7,8},{8,9},{9,10},{10,1... | collective-permute-start | bytes 3833864 | tf_op jit(solution)/shard_map/ppermute | solution.py:18
  307.5 11.9 %collective-permute-done.14 = bf16[128,4992]{0,1:T(8,128)(2,1)} collective-permute-done((bf16[128,4992]{0,1:T(8,128)(2,1)}, bf16[128,4992]{0,1:T(8,128)(2,1)}, u32[]{:S(2)}, u32[]{:S(2)}) %collective-permute-start.14) | collective-permute-done | bytes 1277984 | tf_op jit(solution)/shard_map/ppermute | solution.py:18
  319.4 6.4 %collective-permute-start.15 = (bf16[128,4992]{0,1:T(8,128)(2,1)}, bf16[128,4992]{0,1:T(8,128)(2,1)}, u32[]{:S(2)}, u32[]{:S(2)}) collective-permute-start(bf16[128,4992]{0,1:T(8,128)(2,1)} %collective-permute-done.14), channel_id=1, source_target_pairs={{0,1},{1,2},{2,3},{3,4},{4,5},{5,6},{6,7},{7,8},{8,9},{9,10},{10,1... | collective-permute-start | bytes 3833864 | tf_op jit(solution)/shard_map/ppermute | solution.py:18
  326.2 13.9 %collective-permute-done.15 = bf16[128,4992]{0,1:T(8,128)(2,1)} collective-permute-done((bf16[128,4992]{0,1:T(8,128)(2,1)}, bf16[128,4992]{0,1:T(8,128)(2,1)}, u32[]{:S(2)}, u32[]{:S(2)}) %collective-permute-start.15) | collective-permute-done | bytes 1277984 | tf_op jit(solution)/shard_map/ppermute | solution.py:18
  353.4 7.2 %copy-done = bf16[2176,4992]{0,1:T(8,128)(2,1)} copy-done((bf16[2176,4992]{0,1:T(8,128)(2,1)}, bf16[2176,4992]{0,1:T(8,128)(2,1)S(1)}, u32[]{:S(2)}) %copy-start) | copy-done | bytes 21725208
  362.9 10.4 %while.14 = (s32[]{:T(128)}, bf16[2176,896]{0,1:T(8,128)(2,1)}, s32[4,2]{0,1:T(2,128)S(1)}, bf16[4,128,896]{2,1,0:T(8,128)(2,1)S(1)}, s32[]{:T(128)}) while((s32[]{:T(128)}, bf16[2176,896]{0,1:T(8,128)(2,1)}, s32[4,2]{0,1:T(2,128)S(1)}, bf16[4,128,896]{2,1,0:T(8,128)(2,1)S(1)}, s32[]{:T(128)}) %tuple.60), condition=%wide.while_cond, body=%wide.while_body.sunk | while | flops 2 | bytes 1376353 | solution.py:90
  373.3 7.8 %convolution_convert_fusion = bf16[512,4096]{1,0:T(8,128)(2,1)S(1)} fusion(bf16[512,896]{1,0:T(8,128)(2,1)S(1)} %bitcast.71, bf16[896,4096]{1,0:T(8,128)(2,1)} %param.15), kind=kOutput, calls=%fused_computation.24 | convolution fusion | flops 3760193536 | bytes 12451840 | tf_op jit(solution)/shard_map/dot_general | solution.py:93
  397.2 6.4 %collective-permute-start.17 = (f32[64,2048]{1,0:T(8,128)}, f32[64,2048]{1,0:T(8,128)}, u32[]{:S(2)}, u32[]{:S(2)}) collective-permute-start(f32[64,2048]{1,0:T(8,128)} %bitcast.39), channel_id=1, source_target_pairs={{0,1},{1,2},{2,3},{3,4},{4,5},{5,6},{6,7},{7,8},{8,9},{9,10},{10,1... | collective-permute-start | bytes 1572872 | tf_op jit(solution)/shard_map/ppermute | solution.py:18
  403.6 65.3 %while.15 = (s32[]{:T(128)}, f32[4,128,512]{1,2,0:T(8,128)}, s32[4]{0:T(128)S(1)}, bf16[2176,4992]{0,1:T(8,128)(2,1)}, bf16[128,2048]{1,0:T(8,128)(2,1)}, /*inde...) while((s32[]{:T(128)}, f32[4,128,512]{1,2,0:T(8,128)}, ...), condition=%wide.region_3.4_spmd.clone, body=%wide.region_0.3_spmd.clone.sunk | while | flops 579340416 | bytes 24288636 | solution.py:65
  (179 shorter events, 204.7 us)
Async XLA Ops:
  1.4 303.5 %copy-start.26 = (bf16[128,2048]{1,0:T(8,128)(2,1)S(1)}, bf16[128,2048]{1,0:T(8,128)(2,1)}, u32[]{:S(2)}) copy-start(bf16[128,2048]{1,0:T(8,128)(2,1)} %param.13) | copy-start | bytes 1572868
  2.8 323.0 %copy-start.28 = (s32[2,2]{1,0:T(2,128)S(1)}, s32[2,2]{1,0:T(2,128)}, u32[]{:S(2)}) copy-start(s32[2,2]{1,0:T(2,128)} %param.17) | copy-start | bytes 52
  2.8 323.2 %copy-start.29 = (s32[2]{0:T(128)S(1)}, s32[2]{0:T(128)}, u32[]{:S(2)}) copy-start(s32[2]{0:T(128)} %param.16) | copy-start | bytes 28
  3.1 17.9 %collective-permute-start = (bf16[128,4992]{0,1:T(8,128)(2,1)S(1)}, bf16[128,4992]{0,1:T(8,128)(2,1)S(1)}, u32[]{:S(2)}, u32[]{:S(2)}) collective-permute-start(bf16[128,4992]{0,1:T(8,128)(2,1)S(1)} %pad_maximum_fusion), channel_id=1, source_target_pairs={{0,1},{1,2},{2,3},{3,4},{4,5},{5,6},{6,7},{7,8},{8,9},{9,10},{10,1... | collective-permute-start | bytes 3833864 | tf_op jit(solution)/shard_map/ppermute | solution.py:18
  20.9 20.4 %collective-permute-start.1 = (bf16[128,4992]{0,1:T(8,128)(2,1)S(1)}, bf16[128,4992]{0,1:T(8,128)(2,1)S(1)}, u32[]{:S(2)}, u32[]{:S(2)}) collective-permute-start(bf16[128,4992]{0,1:T(8,128)(2,1)S(1)} %collective-permute-done), channel_id=1, source_target_pairs={{0,1},{1,2},{2,3},{3,4},{4,5},{5,6},{6,7},{7,8},{8,9},{9,10},{10,1... | collective-permute-start | bytes 3833864 | tf_op jit(solution)/shard_map/ppermute | solution.py:18
  42.4 20.4 %collective-permute-start.2 = (bf16[128,4992]{0,1:T(8,128)(2,1)S(1)}, bf16[128,4992]{0,1:T(8,128)(2,1)S(1)}, u32[]{:S(2)}, u32[]{:S(2)}) collective-permute-start(bf16[128,4992]{0,1:T(8,128)(2,1)S(1)} %collective-permute-done.1), channel_id=1, source_target_pairs={{0,1},{1,2},{2,3},{3,4},{4,5},{5,6},{6,7},{7,8},{8,9},{9,10},{10,1... | collective-permute-start | bytes 3833864 | tf_op jit(solution)/shard_map/ppermute | solution.py:18
  63.8 20.4 %collective-permute-start.3 = (bf16[128,4992]{0,1:T(8,128)(2,1)S(1)}, bf16[128,4992]{0,1:T(8,128)(2,1)S(1)}, u32[]{:S(2)}, u32[]{:S(2)}) collective-permute-start(bf16[128,4992]{0,1:T(8,128)(2,1)S(1)} %collective-permute-done.2), channel_id=1, source_target_pairs={{0,1},{1,2},{2,3},{3,4},{4,5},{5,6},{6,7},{7,8},{8,9},{9,10},{10,1... | collective-permute-start | bytes 3833864 | tf_op jit(solution)/shard_map/ppermute | solution.py:18
  85.2 20.4 %collective-permute-start.4 = (bf16[128,4992]{0,1:T(8,128)(2,1)S(1)}, bf16[128,4992]{0,1:T(8,128)(2,1)S(1)}, u32[]{:S(2)}, u32[]{:S(2)}) collective-permute-start(bf16[128,4992]{0,1:T(8,128)(2,1)S(1)} %collective-permute-done.3), channel_id=1, source_target_pairs={{0,1},{1,2},{2,3},{3,4},{4,5},{5,6},{6,7},{7,8},{8,9},{9,10},{10,1... | collective-permute-start | bytes 3833864 | tf_op jit(solution)/shard_map/ppermute | solution.py:18
  106.7 20.4 %collective-permute-start.5 = (bf16[128,4992]{0,1:T(8,128)(2,1)S(1)}, bf16[128,4992]{0,1:T(8,128)(2,1)S(1)}, u32[]{:S(2)}, u32[]{:S(2)}) collective-permute-start(bf16[128,4992]{0,1:T(8,128)(2,1)S(1)} %collective-permute-done.4), channel_id=1, source_target_pairs={{0,1},{1,2},{2,3},{3,4},{4,5},{5,6},{6,7},{7,8},{8,9},{9,10},{10,1... | collective-permute-start | bytes 3833864 | tf_op jit(solution)/shard_map/ppermute | solution.py:18
  128.1 20.4 %collective-permute-start.6 = (bf16[128,4992]{0,1:T(8,128)(2,1)S(1)}, bf16[128,4992]{0,1:T(8,128)(2,1)S(1)}, u32[]{:S(2)}, u32[]{:S(2)}) collective-permute-start(bf16[128,4992]{0,1:T(8,128)(2,1)S(1)} %collective-permute-done.5), channel_id=1, source_target_pairs={{0,1},{1,2},{2,3},{3,4},{4,5},{5,6},{6,7},{7,8},{8,9},{9,10},{10,1... | collective-permute-start | bytes 3833864 | tf_op jit(solution)/shard_map/ppermute | solution.py:18
  149.5 20.4 %collective-permute-start.7 = (bf16[128,4992]{0,1:T(8,128)(2,1)S(1)}, bf16[128,4992]{0,1:T(8,128)(2,1)S(1)}, u32[]{:S(2)}, u32[]{:S(2)}) collective-permute-start(bf16[128,4992]{0,1:T(8,128)(2,1)S(1)} %collective-permute-done.6), channel_id=1, source_target_pairs={{0,1},{1,2},{2,3},{3,4},{4,5},{5,6},{6,7},{7,8},{8,9},{9,10},{10,1... | collective-permute-start | bytes 3833864 | tf_op jit(solution)/shard_map/ppermute | solution.py:18
  171.0 20.4 %collective-permute-start.8 = (bf16[128,4992]{0,1:T(8,128)(2,1)S(1)}, bf16[128,4992]{0,1:T(8,128)(2,1)S(1)}, u32[]{:S(2)}, u32[]{:S(2)}) collective-permute-start(bf16[128,4992]{0,1:T(8,128)(2,1)S(1)} %collective-permute-done.7), channel_id=1, source_target_pairs={{0,1},{1,2},{2,3},{3,4},{4,5},{5,6},{6,7},{7,8},{8,9},{9,10},{10,1... | collective-permute-start | bytes 3833864 | tf_op jit(solution)/shard_map/ppermute | solution.py:18
  192.4 20.4 %collective-permute-start.9 = (bf16[128,4992]{0,1:T(8,128)(2,1)S(1)}, bf16[128,4992]{0,1:T(8,128)(2,1)S(1)}, u32[]{:S(2)}, u32[]{:S(2)}) collective-permute-start(bf16[128,4992]{0,1:T(8,128)(2,1)S(1)} %collective-permute-done.8), channel_id=1, source_target_pairs={{0,1},{1,2},{2,3},{3,4},{4,5},{5,6},{6,7},{7,8},{8,9},{9,10},{10,1... | collective-permute-start | bytes 3833864 | tf_op jit(solution)/shard_map/ppermute | solution.py:18
  213.9 20.4 %collective-permute-start.10 = (bf16[128,4992]{0,1:T(8,128)(2,1)S(1)}, bf16[128,4992]{0,1:T(8,128)(2,1)S(1)}, u32[]{:S(2)}, u32[]{:S(2)}) collective-permute-start(bf16[128,4992]{0,1:T(8,128)(2,1)S(1)} %collective-permute-done.9), channel_id=1, source_target_pairs={{0,1},{1,2},{2,3},{3,4},{4,5},{5,6},{6,7},{7,8},{8,9},{9,10},{10,1... | collective-permute-start | bytes 3833864 | tf_op jit(solution)/shard_map/ppermute | solution.py:18
  235.3 20.4 %collective-permute-start.11 = (bf16[128,4992]{0,1:T(8,128)(2,1)S(1)}, bf16[128,4992]{0,1:T(8,128)(2,1)S(1)}, u32[]{:S(2)}, u32[]{:S(2)}) collective-permute-start(bf16[128,4992]{0,1:T(8,128)(2,1)S(1)} %collective-permute-done.10), channel_id=1, source_target_pairs={{0,1},{1,2},{2,3},{3,4},{4,5},{5,6},{6,7},{7,8},{8,9},{9,10},{10,1... | collective-permute-start | bytes 3833864 | tf_op jit(solution)/shard_map/ppermute | solution.py:18
  256.8 20.4 %collective-permute-start.12 = (bf16[128,4992]{0,1:T(8,128)(2,1)S(1)}, bf16[128,4992]{0,1:T(8,128)(2,1)S(1)}, u32[]{:S(2)}, u32[]{:S(2)}) collective-permute-start(bf16[128,4992]{0,1:T(8,128)(2,1)S(1)} %collective-permute-done.11), channel_id=1, source_target_pairs={{0,1},{1,2},{2,3},{3,4},{4,5},{5,6},{6,7},{7,8},{8,9},{9,10},{10,1... | collective-permute-start | bytes 3833864 | tf_op jit(solution)/shard_map/ppermute | solution.py:18
  278.2 20.4 %collective-permute-start.13 = (bf16[128,4992]{0,1:T(8,128)(2,1)S(1)}, bf16[128,4992]{0,1:T(8,128)(2,1)}, u32[]{:S(2)}, u32[]{:S(2)}) collective-permute-start(bf16[128,4992]{0,1:T(8,128)(2,1)S(1)} %collective-permute-done.12), channel_id=1, source_target_pairs={{0,1},{1,2},{2,3},{3,4},{4,5},{5,6},{6,7},{7,8},{8,9},{9,10},{10,1... | collective-permute-start | bytes 3833864 | tf_op jit(solution)/shard_map/ppermute | solution.py:18
  298.5 20.8 %collective-permute-start.14 = (bf16[128,4992]{0,1:T(8,128)(2,1)}, bf16[128,4992]{0,1:T(8,128)(2,1)}, u32[]{:S(2)}, u32[]{:S(2)}) collective-permute-start(bf16[128,4992]{0,1:T(8,128)(2,1)} %collective-permute-done.13), channel_id=1, source_target_pairs={{0,1},{1,2},{2,3},{3,4},{4,5},{5,6},{6,7},{7,8},{8,9},{9,10},{10,1... | collective-permute-start | bytes 3833864 | tf_op jit(solution)/shard_map/ppermute | solution.py:18
  305.6 20.5 %collective-permute-start.16 = (bf16[64,2048]{1,0:T(8,128)(2,1)}, bf16[64,2048]{1,0:T(8,128)(2,1)S(1)}, u32[]{:S(2)}, u32[]{:S(2)}) collective-permute-start(bf16[64,2048]{1,0:T(8,128)(2,1)} %get-tuple-element.155), channel_id=1, source_target_pairs={{1,0},{2,1},{3,2},{4,3},{5,4},{6,5},{7,6},{8,7},{9,8},{10,9},{11,1... | collective-permute-start | bytes 786440 | tf_op jit(solution)/shard_map/ppermute | solution.py:18
  319.4 20.7 %collective-permute-start.15 = (bf16[128,4992]{0,1:T(8,128)(2,1)}, bf16[128,4992]{0,1:T(8,128)(2,1)}, u32[]{:S(2)}, u32[]{:S(2)}) collective-permute-start(bf16[128,4992]{0,1:T(8,128)(2,1)} %collective-permute-done.14), channel_id=1, source_target_pairs={{0,1},{1,2},{2,3},{3,4},{4,5},{5,6},{6,7},{7,8},{8,9},{9,10},{10,1... | collective-permute-start | bytes 3833864 | tf_op jit(solution)/shard_map/ppermute | solution.py:18
  341.6 3.4 copy-start.25
  353.4 7.3 %copy-start = (bf16[2176,4992]{0,1:T(8,128)(2,1)}, bf16[2176,4992]{0,1:T(8,128)(2,1)S(1)}, u32[]{:S(2)}) copy-start(bf16[2176,4992]{0,1:T(8,128)(2,1)S(1)} %constant_dynamic-update-slice_fusion.1) | copy-start | bytes 65175556
  389.3 4.0 copy-start.1
  397.2 73.8 %collective-permute-start.17 = (f32[64,2048]{1,0:T(8,128)}, f32[64,2048]{1,0:T(8,128)}, u32[]{:S(2)}, u32[]{:S(2)}) collective-permute-start(f32[64,2048]{1,0:T(8,128)} %bitcast.39), channel_id=1, source_target_pairs={{0,1},{1,2},{2,3},{3,4},{4,5},{5,6},{6,7},{7,8},{8,9},{9,10},{10,1... | collective-permute-start | bytes 1572872 | tf_op jit(solution)/shard_map/ppermute | solution.py:18
  (25 other events, 33.9 us)
where the time goes:
time: 475 us; the launch traced here: 473 us
  waiting for transfers between devices  224 us (47%)
  starting transfers between devices  105 us (22%)
  local copies, waits for them, and re-layouts  86.5 us (18%)
  matrix products  49.9 us (11%)
    ppermute x18, waiting for transfers between devices, shifted(): lax.ppermute(value, axis, [(source, source + steps) for source in range(f...  224 us
    ppermute x18, starting transfers between devices, shifted(): lax.ppermute(value, axis, [(source, source + steps) for source in range(f...  105 us
    unnamed x86, local copies, waits for them, and re-layouts  43.6 us
    sub x5, matrix products, masked_weights(): exponent = jnp.where(valid_mask, jnp.exp(masked - largest), 0.0)  27.1 us
    dynamic_slice x4, local copies, waits for them, and re-layouts, one_group(): lax.dynamic_slice_in_dim(window_rows, column_start, group_width, 1)  15.8 us
    dot_general x4, matrix products, one_group(): jnp.einsum('hri,ihd->rhd', weights, value_group, preferred_element_type=j...  12.5 us
    gather x20, local copies, waits for them, and re-layouts  10.3 us
  transfers between devices with their start and end apart: 18, of which 16 were waited for; matrix products, arithmetic and copies ran while one was open for 14% of the time, Pallas kernels for 0%

commit v1 on v0

v1 whole, which is shorter than its diff:
```python
import functools

import jax
import jax.numpy as jnp
from jax import lax
from jax.experimental import pallas as pl
from jax.experimental.pallas import tpu as pltpu
from jax.sharding import PartitionSpec as P

HEAD_DIM = 128
SPAN = 64
REACH = 16
MASKED_SCORE = -1e30
LOG2E = 1.4426950408889634

ENC, Q_OWN, K_OWN, V_OWN, K_PREV, V_PREV, CQ, META, META_PREV = range(9)
PK_OWN, PV_OWN, PK_PREV, PV_PREV, OUT, KINDS = range(9, 15)
LOCAL_W, LOCAL_E, LOCAL_META, LOCALS = range(4)


def dot_t(a, b):
    return lax.dot_general(a, b, (((1,), (1,)), ((), ())), preferred_element_type=jnp.float32)


def kernel(
    group,
    chunks,
    span_count,
    q_in,
    k_in,
    v_in,
    cq_in,
    e_in,
    w_in,
    meta_in,
    out,
    qs,
    ks,
    vs,
    cqs,
    meta_v,
    meta_s,
    enc_own,
    enc_prev,
    weight,
    proj_own,
    proj_prev,
    pks,
    pvs,
    self_out,
    stage,
    send,
    recv,
    local,
):
    tok = q_in.shape[0]
    width = q_in.shape[1]
    window = group * tok
    me = lax.axis_index("ctx")
    chunk = lax.div(me, group)
    off = lax.rem(me, group)
    scale = LOG2E * HEAD_DIM ** (-0.5)
    has_prev = chunk > 0
    has_next = chunk < chunks - 1

    def own_peer(step):
        return lax.rem(off + step, group)

    def columns(index):
        return pl.ds(pl.multiple_of(index * HEAD_DIM, HEAD_DIM), HEAD_DIM)

    def rows(index, base=0):
        return pl.ds(pl.multiple_of(base + index * tok, tok), tok)

    def remote(src, dst, kind, device):
        pltpu.make_async_remote_copy(
            src_ref=src,
            dst_ref=dst,
            send_sem=send.at[kind],
            recv_sem=recv.at[kind],
            device_id={"ctx": device},
            device_id_type=pl.DeviceIdType.MESH,
        ).start()

    def arrived(region, kind):
        pltpu.make_async_copy(region, region, recv.at[kind]).wait()

    def sent(region, kind):
        pltpu.make_async_copy(region, region, send.at[kind]).wait()

    load_w = pltpu.make_async_copy(w_in, weight, local.at[LOCAL_W])
    load_e = pltpu.make_async_copy(e_in, enc_own, local.at[LOCAL_E])
    load_e.start()
    load_w.start()

    barrier = pltpu.get_barrier_semaphore()

    def greet(device):
        pl.semaphore_signal(
            barrier, inc=1, device_id={"ctx": device}, device_id_type=pl.DeviceIdType.MESH
        )

    @pl.loop(1, group)
    def _(step):
        greet(chunk * group + own_peer(step))

    @pl.when(has_prev)
    def _():
        @pl.loop(0, group)
        def _(step):
            greet((chunk - 1) * group + own_peer(step))

    @pl.when(has_next)
    def _():
        @pl.loop(0, group)
        def _(step):
            greet((chunk + 1) * group + own_peer(step))

    friends = group - 1 + jnp.where(has_prev, group, 0) + jnp.where(has_next, group, 0)
    pl.semaphore_wait(barrier, friends)

    @pl.when(has_next)
    def _():
        remote(e_in, enc_prev, ENC, (chunk + 1) * group + off)

    @pl.loop(0, group)
    def _(step):
        peer = own_peer(step)
        cols = columns(peer)

        @pl.when(has_next)
        def _():
            target = (chunk + 1) * group + peer
            remote(k_in.at[:, cols], ks.at[rows(off)], K_PREV, target)
            remote(v_in.at[:, cols], vs.at[rows(off)], V_PREV, target)

        @pl.when(step > 0)
        def _():
            target = chunk * group + peer
            remote(k_in.at[:, cols], ks.at[rows(off, window)], K_OWN, target)
            remote(v_in.at[:, cols], vs.at[rows(off, window)], V_OWN, target)
            remote(q_in.at[:, cols], qs.at[rows(off)], Q_OWN, target)

    def own_copy(src, dst, kind):
        pltpu.make_async_copy(src, dst, recv.at[kind]).start()

    mine = columns(off)
    own_copy(k_in.at[:, mine], ks.at[rows(off, window)], K_OWN)
    own_copy(v_in.at[:, mine], vs.at[rows(off, window)], V_OWN)
    own_copy(q_in.at[:, mine], qs.at[rows(off)], Q_OWN)
    own_copy(cq_in.at[:, mine], cqs.at[rows(off)], CQ)
    own_meta = pl.ds(pl.multiple_of(8 * (off + 1), 8), 8)
    own_copy(meta_in, meta_v.at[own_meta], META)

    @pl.when(has_next & (off == group - 1))
    def _():
        @pl.loop(0, group)
        def _(step):
            remote(meta_in, meta_v.at[pl.ds(0, 8)], META_PREV, (chunk + 1) * group + own_peer(step))

    @pl.loop(1, group)
    def _(step):
        peer = own_peer(step)
        target = chunk * group + peer
        remote(cq_in.at[:, columns(peer)], cqs.at[rows(off)], CQ, target)
        remote(meta_in, meta_v.at[own_meta], META, target)

    load_w.wait()
    load_e.wait()

    def project(encoded, proj, base, key_kind, value_kind):
        @pl.loop(0, group // 2)
        def _(step):
            pair = lax.rem(lax.div(off, 2) + step, group // 2)
            for part, (dst, kind) in enumerate(((pks, key_kind), (pvs, value_kind))):
                start = pl.multiple_of(part * width + pair * 2 * HEAD_DIM, 2 * HEAD_DIM)
                both = pl.ds(start, 2 * HEAD_DIM)
                proj[:, both] = jnp.dot(
                    encoded[...], weight[:, both], preferred_element_type=jnp.float32
                ).astype(jnp.bfloat16)
                for half in range(2):
                    peer = pair * 2 + half
                    cols = pl.ds(pl.multiple_of(part * width + peer * HEAD_DIM, HEAD_DIM), HEAD_DIM)

                    @pl.when(peer != off)
                    def _():
                        remote(proj.at[:, cols], dst.at[rows(off, base)], kind, chunk * group + peer)

                    @pl.when(peer == off)
                    def _():
                        own_copy(proj.at[:, cols], dst.at[rows(off, base)], kind)

    project(enc_own, proj_own, window, PK_OWN, PV_OWN)

    @pl.when(has_prev)
    def _():
        arrived(enc_prev, ENC)
        project(enc_prev, proj_prev, 0, PK_PREV, PV_PREV)

    first_half = pl.ds(0, window)
    second_half = pl.ds(window, window)

    @pl.when(jnp.logical_not(has_prev))
    def _():
        ks[first_half, :] = jnp.zeros((window, HEAD_DIM), jnp.bfloat16)
        vs[first_half, :] = jnp.zeros((window, HEAD_DIM), jnp.bfloat16)
        pks[first_half, :] = jnp.zeros((window, HEAD_DIM), jnp.bfloat16)
        pvs[first_half, :] = jnp.zeros((window, HEAD_DIM), jnp.bfloat16)
        meta_v[pl.ds(0, 8), :] = jnp.zeros((8, meta_v.shape[1]), jnp.int32)

    arrived(qs, Q_OWN)
    arrived(ks.at[second_half], K_OWN)
    arrived(vs.at[second_half], V_OWN)

    @pl.when(has_prev)
    def _():
        arrived(ks.at[first_half], K_PREV)
        arrived(vs.at[first_half], V_PREV)

    tile = 2 * tok
    reach = window + tile

    @pl.loop(0, window // tile)
    def _(index):
        start = pl.multiple_of(index * tile, tile)
        queries = qs[pl.ds(start, tile), :]
        keys = ks[pl.ds(start, reach), :]
        values = vs[pl.ds(start, reach), :]
        least = jnp.where(has_prev, 0, window - start)
        scores = dot_t(queries, keys)
        row = lax.broadcasted_iota(jnp.int32, (tile, tile), 0)
        col = lax.broadcasted_iota(jnp.int32, (tile, tile), 1)
        mid = lax.broadcasted_iota(jnp.int32, (1, window - tile), 1) + tile
        head = jnp.where((col > row) & (col >= least), scores[:, :tile], MASKED_SCORE)
        body = jnp.where(mid >= least, scores[:, tile:window], MASKED_SCORE)
        tail = jnp.where(col <= row, scores[:, window:], MASKED_SCORE)
        scores = jnp.concatenate([head, body, tail], axis=1)
        largest = jnp.max(scores, axis=-1, keepdims=True)
        exponent = jnp.exp2((scores - largest) * scale)
        total = jnp.sum(exponent, axis=-1, keepdims=True)
        result = jnp.dot(exponent.astype(jnp.bfloat16), values, preferred_element_type=jnp.float32)
        self_out[pl.ds(start, tile), :] = result / total

    arrived(meta_v.at[pl.ds(8, 8 * group)], META)
    arrived(cqs, CQ)
    arrived(pks.at[second_half], PK_OWN)
    arrived(pvs.at[second_half], PV_OWN)

    @pl.when(has_prev)
    def _():
        arrived(meta_v.at[pl.ds(0, 8)], META_PREV)
        arrived(pks.at[first_half], PK_PREV)
        arrived(pvs.at[first_half], PV_PREV)

    to_scalar = pltpu.make_async_copy(meta_v, meta_s, local.at[LOCAL_META])
    to_scalar.start()
    to_scalar.wait()

    @pl.loop(0, window // tile)
    def _(index):
        start = pl.multiple_of(index * tile, tile)
        lowest = pl.multiple_of(start + SPAN, SPAN)
        across = window + tile - 2 * SPAN
        keys = pks[pl.ds(lowest, across), :]
        values = pvs[pl.ds(lowest, across), :]
        scores = dot_t(cqs[pl.ds(start, tile), :], keys)
        place = lax.broadcasted_iota(jnp.int32, (1, across), 1) + lowest
        parts, totals = [], []
        for piece in range(tile // SPAN):
            span = index * (tile // SPAN) + piece
            entry = span + span_count - 1
            block = lax.div(entry, span_count) * 8
            lane = lax.rem(entry, span_count) * 3
            real = has_prev | (span > 0)
            count = jnp.where(real, meta_s[block, lane], 0)
            times = jnp.zeros((1, across), jnp.float32)
            for slot in range(2):
                first = meta_s[block, lane + 1 + slot] * SPAN - (chunk - 1) * window
                first = jnp.where(slot < count, first, -4 * window)
                inside = (place >= first) & (place < first + 2 * SPAN)
                times = times + jnp.where(inside, 1.0, 0.0)
            piece_scores = scores[piece * SPAN : (piece + 1) * SPAN]
            piece_scores = jnp.where(times > 0.0, piece_scores, MASKED_SCORE)
            largest = jnp.max(piece_scores, axis=-1, keepdims=True)
            exponent = jnp.exp2((piece_scores - largest) * scale) * times
            total = jnp.sum(exponent, axis=-1, keepdims=True)
            totals.append(total + jnp.where(count > 0, 0.0, 1.0))
            parts.append(exponent.astype(jnp.bfloat16))
        result = jnp.dot(
            jnp.concatenate(parts, axis=0), values, preferred_element_type=jnp.float32
        ) / jnp.concatenate(totals, axis=0)
        both = self_out[pl.ds(start, tile), :] + result
        stage[pl.ds(start, tile), :] = both.astype(jnp.bfloat16)
        for half in range(tile // tok):
            owner = index * (tile // tok) + half

            @pl.when(owner != off)
            def _():
                remote(stage.at[rows(owner)], out.at[:, mine], OUT, chunk * group + owner)

            @pl.when(owner == off)
            def _():
                own_copy(stage.at[rows(owner)], out.at[:, mine], OUT)

    arrived(out, OUT)

    others = pl.ds(0, (group - 1) * tok)
    for region, kind in (
        (qs, Q_OWN),
        (ks, K_OWN),
        (vs, V_OWN),
        (cqs, CQ),
        (pks, PK_OWN),
        (pvs, PV_OWN),
        (stage, OUT),
    ):
        sent(region.at[others], kind)
    sent(meta_v.at[pl.ds(0, 8 * (group - 1))], META)

    @pl.when(has_prev)
    def _():
        sent(pks.at[others], PK_PREV)
        sent(pvs.at[others], PV_PREV)

    @pl.when(has_next)
    def _():
        sent(enc_prev, ENC)
        sent(ks.at[first_half], K_PREV)
        sent(vs.at[first_half], V_PREV)

    @pl.when(has_next & (off == group - 1))
    def _():
        sent(meta_v.at[pl.ds(0, 8 * group)], META_PREV)


def per_device(
    queries, self_keys, self_values, cross_queries, encoded, neighbour_weight, counts, sources
):
    tok, width = queries.shape
    depth = encoded.shape[1]
    group = width // HEAD_DIM
    assert group == REACH
    chunks = lax.axis_size("ctx") // group
    window = group * tok
    span_count = counts.shape[0]
    meta = jnp.concatenate([counts[:, None], sources], axis=1).reshape(1, -1)
    meta = jnp.pad(meta, ((0, 7), (0, HEAD_DIM - meta.shape[1])))
    bf16 = jnp.bfloat16
    anywhere = pl.BlockSpec(memory_space=pl.ANY)
    return pl.pallas_call(
        functools.partial(kernel, group, chunks, span_count),
        out_shape=jax.ShapeDtypeStruct((tok, width), bf16),
        in_specs=[anywhere] * 7,
        out_specs=anywhere,
        scratch_shapes=[
            pltpu.VMEM((window, HEAD_DIM), bf16),
            pltpu.VMEM((2 * window, HEAD_DIM), bf16),
            pltpu.VMEM((2 * window, HEAD_DIM), bf16),
            pltpu.VMEM((window, HEAD_DIM), bf16),
            pltpu.VMEM((8 * (group + 1), HEAD_DIM), jnp.int32),
            pltpu.SMEM((8 * (group + 1), HEAD_DIM), jnp.int32),
            pltpu.VMEM((tok, depth), bf16),
            pltpu.VMEM((tok, depth), bf16),
            pltpu.VMEM((depth, 2 * width), bf16),
            pltpu.VMEM((tok, 2 * width), bf16),
            pltpu.VMEM((tok, 2 * width), bf16),
            pltpu.VMEM((2 * window, HEAD_DIM), bf16),
            pltpu.VMEM((2 * window, HEAD_DIM), bf16),
            pltpu.VMEM((window, HEAD_DIM), jnp.float32),
            pltpu.VMEM((window, HEAD_DIM), bf16),
            pltpu.SemaphoreType.DMA((KINDS,)),
            pltpu.SemaphoreType.DMA((KINDS,)),
            pltpu.SemaphoreType.DMA((LOCALS,)),
        ],
        compiler_params=pltpu.CompilerParams(
            collective_id=0, has_side_effects=True, vmem_limit_bytes=48 * 2**20
        ),
        cost_estimate=pl.CostEstimate(
            flops=4 * window * (window + 2 * tok) * HEAD_DIM,
            bytes_accessed=8 * window * HEAD_DIM * 2,
            transcendentals=window * window,
        ),
    )(queries, self_keys, self_values, cross_queries, encoded, neighbour_weight, meta)


def solution(mesh):
    return jax.shard_map(
        per_device,
        mesh=mesh,
        in_specs=(
            P(("groups", "ctx"), None),
            P(("groups", "ctx"), None),
            P(("groups", "ctx"), None),
            P(("groups", "ctx"), None),
            P(("groups", "ctx"), None),
            P(),
            P(("groups", "ctx")),
            P(("groups", "ctx"), None),
        ),
        out_specs=P(("groups", "ctx"), None),
        check_vma=False,
    )
```

time: 475 us -> 107 us (0.23)
  the two profiles are of different devices: /device:TPU:7 before, /device:TPU:29 now
where the time goes in v1:
time: 107 us
  Pallas kernels  99.4 us (93%)
  local copies, waits for them, and re-layouts  6.73 us (6%)
    pallas_call x1, Pallas kernels, per_device(): pl.pallas_call(functools.partial(kernel, group, chunks, span_count), out_...  99.4 us
    unnamed x11, local copies, waits for them, and re-layouts  5.9 us

profile of v1, /device:TPU:29, one launch (start us, length us, event | category | flops | bytes accessed | tf_op | source)
XLA Modules:
  0.0 106.9 jit_solution(17450004859092957183)
XLA Ops:
  0.0 0.7 copy.9
  0.7 0.8 pad_add_fusion
  1.5 0.1 reshape.3
  1.6 0.0 copy-start
  1.6 1.0 copy-done
  2.6 0.0 copy-start.1
  2.6 1.0 copy-done.1
  3.7 0.0 copy-start.2
  3.7 1.0 copy-done.2
  4.7 0.0 copy-start.3
  4.7 1.0 copy-done.3
  5.8 0.0 copy-start.4
  5.8 0.9 copy-done.4
  6.7 99.4 %shard_map.82 = bf16[128,2048]{1,0:T(8,128)(2,1)S(1)} custom-call(bf16[128,2048]{1,0:T(8,128)(2,1)S(1)} %copy-done, bf16[128,2048]{1,0:T(8,128)(2,1)S(1)} %copy-done.1, bf16[128,2048]{1,0:T(8,128)(2,1)S(1)} %copy-done.2, bf16[128,2048]{1,0:T(8,128)(2,1)S(1)} %copy-done.3, bf16[128,896]{1,0:T(8,128)(2,1)S(1)} %copy-done.4, bf16[896,4096]{1,0:T(8,128)(2,1)} %w_in.1, ...), custom_call_target="tpu_custom_call" | custom-call | flops 2415919104 | bytes 4194304 | tf_op jit(solution)/shard_map/pallas_call | solution.py:350
  106.1 0.8 copy.11
  (1 shorter events, 0.0 us)
Async XLA Ops:
  1.6 1.0 copy-start
  2.6 1.0 copy-start.1
  3.7 1.0 copy-start.2
  4.7 1.0 copy-start.3
  5.8 0.9 copy-start.4

commit v2 on v1

--- a/solution.py
+++ b/solution.py
@@ -14,8 +14,8 @@
 LOG2E = 1.4426950408889634
 
 ENC, Q_OWN, K_OWN, V_OWN, K_PREV, V_PREV, CQ, META, META_PREV = range(9)
-PK_OWN, PV_OWN, PK_PREV, PV_PREV, OUT, KINDS = range(9, 15)
-LOCAL_W, LOCAL_E, LOCAL_META, LOCALS = range(4)
+PK_OWN, PV_OWN, PK_PREV, PV_PREV, OUT, ENC_PAIR, ENC_PREV_PAIR, KINDS = range(9, 17)
+LOCAL_WK, LOCAL_WV, LOCAL_E, LOCAL_META, LOCALS = range(5)
 
 
 def dot_t(a, b):
@@ -88,10 +88,24 @@
     def sent(region, kind):
         pltpu.make_async_copy(region, region, send.at[kind]).wait()
 
-    load_w = pltpu.make_async_copy(w_in, weight, local.at[LOCAL_W])
-    load_e = pltpu.make_async_copy(e_in, enc_own, local.at[LOCAL_E])
+    half_heads = group // 2
+    half_width = width // 2
+    half = lax.div(off, half_heads)
+    partner = lax.rem(off + half_heads, group)
+    first_rows = pl.ds(0, tok)
+    pair_rows = pl.ds(tok, tok)
+    load_w = [
+        pltpu.make_async_copy(
+            w_in.at[:, pl.ds(pl.multiple_of(part * width + half * half_width, half_width), half_width)],
+            weight.at[:, pl.ds(part * half_width, half_width)],
+            local.at[LOCAL_WK + part],
+        )
+        for part in range(2)
+    ]
+    load_e = pltpu.make_async_copy(e_in, enc_own.at[first_rows], local.at[LOCAL_E])
     load_e.start()
-    load_w.start()
+    load_w[0].start()
+    load_w[1].start()
 
     barrier = pltpu.get_barrier_semaphore()
 
@@ -121,10 +135,11 @@
 
     @pl.when(has_next)
     def _():
-        remote(e_in, enc_prev, ENC, (chunk + 1) * group + off)
-
-    @pl.loop(0, group)
-    def _(step):
+        remote(e_in, enc_prev.at[first_rows], ENC, (chunk + 1) * group + off)
+
+    remote(e_in, enc_own.at[pair_rows], ENC_PAIR, chunk * group + partner)
+
+    def send_next(step):
         peer = own_peer(step)
         cols = columns(peer)
 
@@ -133,6 +148,17 @@
             target = (chunk + 1) * group + peer
             remote(k_in.at[:, cols], ks.at[rows(off)], K_PREV, target)
             remote(v_in.at[:, cols], vs.at[rows(off)], V_PREV, target)
+
+    early = group // 2
+
+    @pl.loop(0, group)
+    def _(step):
+        peer = own_peer(step)
+        cols = columns(peer)
+
+        @pl.when(step % 2 == 0)
+        def _():
+            send_next(lax.div(step, 2))
 
         @pl.when(step > 0)
         def _():
@@ -165,37 +191,50 @@
         remote(cq_in.at[:, columns(peer)], cqs.at[rows(off)], CQ, target)
         remote(meta_in, meta_v.at[own_meta], META, target)
 
-    load_w.wait()
+    load_w[0].wait()
+    load_w[1].wait()
     load_e.wait()
 
-    def project(encoded, proj, base, key_kind, value_kind):
-        @pl.loop(0, group // 2)
+    def project(encoded, proj, base, key_kind, value_kind, also):
+        @pl.loop(0, half_heads // 2)
         def _(step):
-            pair = lax.rem(lax.div(off, 2) + step, group // 2)
+            pair = lax.rem(lax.div(off, 2) + step, half_heads // 2)
             for part, (dst, kind) in enumerate(((pks, key_kind), (pvs, value_kind))):
-                start = pl.multiple_of(part * width + pair * 2 * HEAD_DIM, 2 * HEAD_DIM)
+                start = pl.multiple_of(part * half_width + pair * 2 * HEAD_DIM, 2 * HEAD_DIM)
                 both = pl.ds(start, 2 * HEAD_DIM)
                 proj[:, both] = jnp.dot(
                     encoded[...], weight[:, both], preferred_element_type=jnp.float32
                 ).astype(jnp.bfloat16)
-                for half in range(2):
-                    peer = pair * 2 + half
-                    cols = pl.ds(pl.multiple_of(part * width + peer * HEAD_DIM, HEAD_DIM), HEAD_DIM)
-
-                    @pl.when(peer != off)
-                    def _():
-                        remote(proj.at[:, cols], dst.at[rows(off, base)], kind, chunk * group + peer)
-
-                    @pl.when(peer == off)
-                    def _():
-                        own_copy(proj.at[:, cols], dst.at[rows(off, base)], kind)
-
-    project(enc_own, proj_own, window, PK_OWN, PV_OWN)
+                for side in range(2):
+                    peer = half * half_heads + pair * 2 + side
+                    start = part * half_width + (pair * 2 + side) * HEAD_DIM
+                    cols = pl.ds(pl.multiple_of(start, HEAD_DIM), HEAD_DIM)
+                    for source, owner in ((first_rows, off), (pair_rows, partner)):
+                        goal = dst.at[rows(owner, base)]
+
+                        @pl.when(peer != off)
+                        def _():
+                            remote(proj.at[source, cols], goal, kind, chunk * group + peer)
+
+                        @pl.when(peer == off)
+                        def _():
+                            own_copy(proj.at[source, cols], goal, kind)
+
+            also(step)
+
+    def send_two(step):
+        send_next(early + 2 * step)
+        send_next(early + 2 * step + 1)
+
+    arrived(enc_own.at[pair_rows], ENC_PAIR)
+    project(enc_own, proj_own, window, PK_OWN, PV_OWN, send_two)
 
     @pl.when(has_prev)
     def _():
-        arrived(enc_prev, ENC)
-        project(enc_prev, proj_prev, 0, PK_PREV, PV_PREV)
+        arrived(enc_prev.at[first_rows], ENC)
+        remote(enc_prev.at[first_rows], enc_prev.at[pair_rows], ENC_PREV_PAIR, chunk * group + partner)
+        arrived(enc_prev.at[pair_rows], ENC_PREV_PAIR)
+        project(enc_prev, proj_prev, 0, PK_PREV, PV_PREV, lambda step: None)
 
     first_half = pl.ds(0, window)
     second_half = pl.ds(window, window)
@@ -310,21 +349,24 @@
         (ks, K_OWN),
         (vs, V_OWN),
         (cqs, CQ),
-        (pks, PK_OWN),
-        (pvs, PV_OWN),
         (stage, OUT),
     ):
         sent(region.at[others], kind)
     sent(meta_v.at[pl.ds(0, 8 * (group - 1))], META)
+    sent(enc_own.at[first_rows], ENC_PAIR)
+    projected = pl.ds(0, 2 * (half_heads - 1) * tok)
+    sent(pks.at[projected], PK_OWN)
+    sent(pvs.at[projected], PV_OWN)
 
     @pl.when(has_prev)
     def _():
-        sent(pks.at[others], PK_PREV)
-        sent(pvs.at[others], PV_PREV)
+        sent(pks.at[projected], PK_PREV)
+        sent(pvs.at[projected], PV_PREV)
+        sent(enc_prev.at[first_rows], ENC_PREV_PAIR)
 
     @pl.when(has_next)
     def _():
-        sent(enc_prev, ENC)
+        sent(enc_prev.at[first_rows], ENC)
         sent(ks.at[first_half], K_PREV)
         sent(vs.at[first_half], V_PREV)
 
@@ -346,7 +388,7 @@
     meta = jnp.concatenate([counts[:, None], sources], axis=1).reshape(1, -1)
     meta = jnp.pad(meta, ((0, 7), (0, HEAD_DIM - meta.shape[1])))
     bf16 = jnp.bfloat16
-    anywhere = pl.BlockSpec(memory_space=pl.ANY)
+    anywhere = pl.BlockSpec(memory_space=pltpu.HBM)
     return pl.pallas_call(
         functools.partial(kernel, group, chunks, span_count),
         out_shape=jax.ShapeDtypeStruct((tok, width), bf16),
@@ -359,11 +401,11 @@
             pltpu.VMEM((window, HEAD_DIM), bf16),
             pltpu.VMEM((8 * (group + 1), HEAD_DIM), jnp.int32),
             pltpu.SMEM((8 * (group + 1), HEAD_DIM), jnp.int32),
-            pltpu.VMEM((tok, depth), bf16),
-            pltpu.VMEM((tok, depth), bf16),
-            pltpu.VMEM((depth, 2 * width), bf16),
-            pltpu.VMEM((tok, 2 * width), bf16),
-            pltpu.VMEM((tok, 2 * width), bf16),
+            pltpu.VMEM((2 * tok, depth), bf16),
+            pltpu.VMEM((2 * tok, depth), bf16),
+            pltpu.VMEM((depth, width), bf16),
+            pltpu.VMEM((2 * tok, width), bf16),
+            pltpu.VMEM((2 * tok, width), bf16),
             pltpu.VMEM((2 * window, HEAD_DIM), bf16),
             pltpu.VMEM((2 * window, HEAD_DIM), bf16),
             pltpu.VMEM((window, HEAD_DIM), jnp.float32),
@@ -373,7 +415,7 @@
             pltpu.SemaphoreType.DMA((LOCALS,)),
         ],
         compiler_params=pltpu.CompilerParams(
-            collective_id=0, has_side_effects=True, vmem_limit_bytes=48 * 2**20
+            collective_id=0, has_side_effects=True, vmem_limit_bytes=63 * 2**20 + 2**19
         ),
         cost_estimate=pl.CostEstimate(
             flops=4 * window * (window + 2 * tok) * HEAD_DIM,

time: 107 us -> 102 us (0.953)
  local copies, waits for them, and re-layouts: 6.73 us -> 3.31 us
  Pallas kernels: 99.4 us -> 97.3 us
    unnamed x11 -> x1, local copies, waits for them, and re-layouts: 5.9 us -> 1.88 us
    pallas_call x1, Pallas kernels: 99.4 us -> 97.3 us  [per_device(): pl.pallas_call(functools.partial(kernel, group, chunks, span_count), out_...]
where the time goes in v2:
time: 102 us; the launch traced here: 101 us
  Pallas kernels  97.3 us (95%)
  local copies, waits for them, and re-layouts  3.31 us (3%)
    pallas_call x1, Pallas kernels, per_device(): pl.pallas_call(functools.partial(kernel, group, chunks, span_count), out_...  97.3 us

profile of v2, /device:TPU:29, one launch (start us, length us, event | category | flops | bytes accessed | tf_op | source)
XLA Modules:
  0.0 101.4 jit_solution(15440050028386501129)
XLA Ops:
  0.0 0.7 copy.9
  0.7 0.8 pad_add_fusion
  1.5 0.1 reshape.3
  1.6 0.6 pad.4.meta_in
  2.2 97.3 %shard_map.82 = bf16[128,2048]{1,0:T(8,128)(2,1)} custom-call(bf16[128,2048]{1,0:T(8,128)(2,1)} %q_in.1, bf16[128,2048]{1,0:T(8,128)(2,1)} %k_in.1, bf16[128,2048]{1,0:T(8,128)(2,1)} %v_in.1, bf16[128,2048]{1,0:T(8,128)(2,1)} %cq_in.1, bf16[128,896]{1,0:T(8,128)(2,1)} %e_in.1, bf16[896,4096]{1,0:T(8,128)(2,1)} %w_in.1, s32[8,128]{1,0:T(8,128)} %pad.4.meta_in), custom_call_target="tpu_custom_call" | custom-call | flops 2415919104 | bytes 4194304 | tf_op jit(solution)/shard_map/pallas_call | solution.py:392
  99.5 1.9 %copy.11 = bf16[128,2048]{1,0:T(8,128)(2,1)} copy(bf16[128,2048]{1,0:T(8,128)(2,1)} %shard_map.82) | data formatting | bytes 1048576
